TPU v7x, 32 devices: a whole 2x2x4 slice. The times are simulated.
32 devices in a mesh: groups: 2 (over x), blk: 16 (over z, y, core).
Axes of the slice: x: 2, y: 2, z: 4, core: 2. Of those that a mesh axis runs over, the one named last changes fastest.
Arguments:
- trans_east: float32 [1024, 16, 128], P(('groups', 'blk')), parts along dimension 0, may hold values from 2 to 20
- trans_north: float32 [1024, 16, 128], P(('groups', 'blk')), parts along dimension 0, may hold values from 0.05 to 3
- trans_up: float32 [1024, 16, 128], P(('groups', 'blk')), parts along dimension 0, may hold values from 0.05 to 3
- storage: float32 [1024, 16, 128], P(('groups', 'blk')), parts along dimension 0, may hold values from 0.2 to 4
- support_reach: int32 [64, 8, 4], P(('groups', 'blk')), parts along dimension 0, may hold values from 1 to 16, as said below
Outputs:
- basis_out: float32 [64, 8, 48, 16, 128], P(('groups', 'blk')), parts along dimension 0
There are 2 independent parts, one for each index of `groups`. A program takes and returns all parts, laid end to end along the dimension named above; each array names one. Nothing has to cross between parts.
Inputs may be any that keep to these rules, and one draw needn't show every extreme that they name: `support_reach`: at least one coarse block reaches the full 16 cells in all four directions.
All inputs are finite; a program needn't handle non-finite values.
Results may differ from a plain program's by a relative error of at most 0.0003.
Values sent between devices are 32-bit elements; how exact they have to be, the bound alone decides.
No kernel may reach another device: no remote copies, remote signals or barrier semaphores. Data moves between devices by JAX's collectives and lax.ppermute only.
A program may use at most 128 MiB of HBM per device.

v0:
```python
import functools

import jax
import jax.numpy as jnp
from jax import lax
from jax.experimental import pallas as pl
from jax.experimental.pallas import tpu as pltpu
from jax.sharding import PartitionSpec as P


TAIL = 8
EARLY = 15
ODD_EARLY = 4


class Lanes:
    def __init__(self, shape, width):
        tile = lax.broadcasted_iota(jnp.int32, (TAIL, shape[1]), 1)

        def rows(v):
            return jnp.concatenate([v] * (shape[0] // TAIL), axis=0)

        self.rows, self.lanes = shape
        self.width = width
        self.lane = rows(tile)
        self.local = rows(lax.rem(tile, width))
        self.first = self.local == 0
        self.last = self.local == width - 1
        self.odd = rows(lax.rem(tile // width, 2)) == 1
        self.row0 = lax.broadcasted_iota(jnp.int32, shape, 0) == 0
        self.lane0 = self.lane == 0

    def around(self, k):
        start = k * self.width - self.width // 2
        return (self.lane >= start) & (self.lane < start + 2 * self.width)

    def zm(self, v):
        return pltpu.roll(v, 1, 1)

    def zp(self, v):
        return pltpu.roll(v, self.lanes - 1, 1)

    def ym(self, v):
        return pltpu.roll(v, 1, 0)

    def yp(self, v):
        return pltpu.roll(v, self.rows - 1, 0)


def reciprocal(x):
    r = pl.reciprocal(x, approx=True)
    return r * (2.0 - x * r)


def within_y(ln, ty):
    ty = jnp.where(ln.row0, 0.0, ty)
    return ty, ln.yp(ty)


def within_z(ln, tz):
    tz = jnp.where(ln.lane0, 0.0, tz)
    return tz, ln.zp(tz)


def cross(ln, ty, tz, s):
    ty, typ = within_y(ln, ty)
    tz, tzp = within_z(ln, tz)
    return s * (1.0 / 3.0) + ((ty + typ) + (tz + tzp)), (ty, typ, tz, tzp)


class Plane:
    def __init__(self, ln, tx, txn, ty, tz, s, valid=None):
        self.ln = ln
        self.tx, self.txn = tx, txn
        e, (self.ty, self.typ, self.tz, self.tzp) = cross(ln, ty, tz, s)
        e = e + (tx + txn)
        if valid is not None:
            e = jnp.where(valid, e, 1.0)
        self.half = 0.5 * e + s * (1.0 / 3.0)
        self.spread(e)

    def spread(self, e):
        ln = self.ln
        self.all = 1.5 * e
        self.q = reciprocal(self.all)
        self.z1 = self.q * jnp.where(ln.first, self.tz, jnp.where(ln.last, self.tzp, 0.0))
        self.zm = ln.zm(self.z1)
        self.zp = ln.zp(self.z1)

    def toward(self, low):
        return self.tx if low else self.txn

    def inward(self, low):
        return self.txn if low else self.tx

    def edge(self, low):
        self.x1 = self.q * self.toward(low)
        self.o1 = 1.0 - self.z1 - self.x1

    def rim(self):
        return self.tz * self.zm + self.tzp * self.zp

    def along_y(self, v):
        return self.ty * self.ln.ym(v) + self.typ * self.ln.yp(v)


class Rim(Plane):
    def __init__(self, ln, e, tz):
        self.ln = ln
        self.tz = jnp.where(ln.lane0, 0.0, tz)
        self.tzp = ln.zp(self.tz)
        self.spread(e)


def plane_at(ln, faces, p):
    return Plane(ln, faces[0, p], faces[0, p + 1], faces[1, p], faces[2, p], faces[3, p])


def middle(p, below, above, mz):
    ln = p.ln
    vz = p.half * p.z1 + p.tx * below.z1 + p.txn * above.z1 + p.along_y(p.z1)
    vz = vz + p.tz * jnp.where(ln.first, 1.0 - p.zm, p.zm)
    vz = vz + p.tzp * jnp.where(ln.last, 1.0 - p.zp, p.zp)
    kept = vz * mz
    return p.all - vz, kept, p.all - (vz - kept)


def second(p, edge, inner, low, mz, mx):
    below, above = (edge, inner) if low else (inner, edge)
    ln = p.ln
    first_o = ln.zm(p.z1)
    vz = p.half * p.z1 + p.tx * below.z1 + p.txn * above.z1 + p.along_y(p.z1)
    vz = vz + p.tz * jnp.where(ln.first, 1.0 - first_o, first_o)
    vz = vz + p.tzp * jnp.where(ln.last, 1.0 - p.zp, p.zp)
    vx = p.toward(low) * edge.x1
    kept_z, kept_x = vz * mz, vx * mx
    total = p.all - (vz - kept_z) - (vx - kept_x)
    return p.all - vz - vx, kept_z, kept_x, total


def edge_own(p, inner_o1, inner_z1, outer_x1, low, mz):
    ln = p.ln
    om, op = ln.zm(p.o1), ln.zp(p.o1)
    vo = p.half * p.o1 + p.toward(low) * outer_x1 + p.inward(low) * inner_o1 + p.along_y(p.o1)
    vo = vo + p.tz * jnp.where(ln.first, p.zm, om) + p.tzp * jnp.where(ln.last, p.zp, op)
    vz = p.half * p.z1 + p.inward(low) * inner_z1 + p.along_y(p.z1)
    vz = vz + p.tz * jnp.where(ln.first, om, p.zm) + p.tzp * jnp.where(ln.last, op, p.zp)
    return vo, vz * mz


def edge_total(p, mz):
    rim = p.rim()
    return p.all - (rim - rim * mz)


def edge_spill(p, own, low):
    ln = p.ln
    xm, xp = ln.zm(p.x1), ln.zp(p.x1)
    face = p.toward(low)
    vx = p.half * p.x1 + face * own.o1 + p.along_y(p.x1)
    vx = vx + p.tz * jnp.where(ln.first, 0.0, xm) + p.tzp * jnp.where(ln.last, 0.0, xp)
    vd = face * own.z1 + p.tz * jnp.where(ln.first, xm, 0.0) + p.tzp * jnp.where(ln.last, xp, 0.0)
    return vx, vd


def store(ln, dst, plane, blocks, own, other, total):
    scale = reciprocal(total)
    own = own * scale
    other = jnp.zeros_like(own) if other is None else other * scale
    even, odd = jnp.where(ln.odd, other, own), jnp.where(ln.odd, own, other)
    for k in range(blocks):
        dst[k, plane] = jnp.where(ln.around(k), odd if k % 2 else even, 0.0)


def work_side(ln, low, valid, faces, masks, msg, put):
    n, rows, lanes = faces.shape[1:]
    layers = masks.shape[0]

    def own(i, j):
        return faces[i, jnp.where(low, j, n - 1 - j)]

    def got(i):
        tiles = rows // TAIL
        return msg[pl.ds(1 + tiles * i, tiles)].reshape(rows, lanes)

    f1, f2, f3 = (faces[0, jnp.where(low, j, n - j)] for j in (1, 2, 3))
    f0 = jnp.where(valid, jnp.where(low, faces[0, 0], got(6)), 0.0)
    g1 = got(0)
    a0 = Plane(ln, f0, f1, own(1, 0), own(2, 0), own(3, 0))
    a1 = Plane(ln, f1, f2, own(1, 1), own(2, 1), own(3, 1))
    a2 = Plane(ln, f2, f3, own(1, 2), own(2, 2), own(3, 2))
    b0 = Plane(ln, g1, f0, got(1), got(2), got(3), valid)
    b1 = Rim(ln, jnp.where(valid, got(4) + g1, 1.0), got(5))
    mine = masks[jnp.where(low, 0, layers - 1)]
    mz, my_reach = mine[0:1], jnp.where(low, mine[1:2], mine[2:3])
    theirs = msg[0]
    mo, their_reach = theirs[0:1], jnp.where(low, theirs[2:3], theirs[1:2])
    a0.edge(True)
    b0.edge(False)
    vx = g1 * b0.x1
    kept = vx * my_reach
    put(0, kept, None, edge_total(b1, mo) - (vx - kept))
    vx, vd = edge_spill(b0, a0, False)
    put(1, vx, vd, edge_total(b0, mo))
    vo, vz = edge_own(a0, 1.0 - a1.z1, a1.z1, b0.x1, True, mz)
    put(2, vo, vz, edge_total(a0, mz))
    vo, vz, _, total = second(a1, a0, a2, True, mz, their_reach)
    put(3, vo, vz, total)


def store_side(ln, buf, low, blocks):
    def put(i, own, other, total):
        store(ln, buf, jnp.where(low, i, 3 - i), blocks, own, other, total)

    return put


def send_one_side(buf, out, low, width, layers, sem, k):
    layer = jnp.where(low, 0, layers - 1)
    start = jnp.where(low, width - 2, 2 * width - 2)
    there = out.at[pl.ds((layer * buf.shape[0] + k) * 3 * width + start, 4)]
    return pltpu.make_async_copy(buf.at[k], there, sem)


def clear_run(zeros, out, b, bases, width, sem):
    depth = width - 2
    ends = isinstance(b, int) and b in (0, bases)
    count = depth if ends else 2 * depth
    start = 0 if ends and b == 0 else b * 3 * width - depth
    return pltpu.make_async_copy(zeros.at[pl.ds(0, count)], out.at[pl.ds(start, count)], sem)


def clear_runs(zeros, out, first, last, bases, width, sem):
    def body(b, _):
        clear_run(zeros, out, b, bases, width, sem).start()

    lax.fori_loop(first, last, body, None)


def wait_planes(out, count, sem):
    some = out.at[pl.ds(0, count)]
    pltpu.make_async_copy(some, some, sem).wait()


def first_early(me, bases):
    return jnp.where(me == 1, bases - EARLY, jnp.where(lax.rem(me, 2) == 1, bases - ODD_EARLY, bases))


def pack_kernel(
    n, width, axis, tx, ty, tz, s, reach, msg_a, msg_b, masks, faces, out,
    held_reach, zeros, buf, read_sems, sem,
):
    layers, _, blocks = held_reach.shape
    rows, lanes = faces.shape[2:]
    fetch = pltpu.make_async_copy(reach, held_reach, read_sems.at[4])
    fetch.start()
    copies = [
        pltpu.make_async_copy(a, faces.at[i], read_sems.at[i]) for i, a in enumerate((tx, ty, tz, s))
    ]
    for i in (1, 2, 0, 3):
        copies[i].start()
    bases = layers * blocks
    me = lax.axis_index(axis)
    late = first_early(me, bases)

    @pl.when(late < bases)
    def _():
        zeros[...] = jnp.zeros(zeros.shape, jnp.float32)
        clear_runs(zeros, out, late, bases, bases, width, sem)

    masks[...] = jnp.zeros(masks.shape, jnp.float32)
    lane = lax.broadcasted_iota(jnp.int32, (4, lanes), 1)
    block = lane // width
    local = lane - block * width
    fetch.wait()
    for layer in range(layers):
        r = jnp.zeros((4, lanes), jnp.int32)
        for k in range(blocks):
            r = jnp.where(block == k, held_reach[layer, :, k : k + 1], r)
        low = pltpu.roll(r, width, 1)
        high = pltpu.roll(r, lanes - width, 1)
        near = jnp.where(
            local[0:1] < width // 2,
            jnp.where(low[3:4] >= local[0:1] + 1, 1.0, 0.0),
            jnp.where(high[2:3] >= width - local[0:1], 1.0, 0.0),
        )
        masks[layer, 0:1] = near
        masks[layer, 1:3] = jnp.where(r[0:2] >= 2, 1.0, 0.0)
    even = lax.rem(me, 2) == 0

    def put(tile, up, down):
        up, down = (v.reshape(-1, TAIL, lanes) for v in (up, down))
        where = pl.ds(tile, up.shape[0])
        msg_a[where] = jnp.where(even, up, down)
        msg_b[where] = jnp.where(even, down, up)

    put(0, masks[layers - 1], masks[0])
    ln = Lanes(faces.shape[2:], width)
    behind = {}

    def plane(slot, up, down):
        put(1 + slot * (rows // TAIL), up, down)

    for i, across in ((1, lambda v: within_y(ln, v)), (2, lambda v: within_z(ln, v))):
        copies[i].wait()
        plane(i, faces[i, n - 1], faces[i, 0])
        for p in (n - 2, 1):
            v, v_next = across(faces[i, p])
            behind[p] = behind.get(p, 0.0) + (v + v_next)
    plane(5, faces[2, n - 2], faces[2, 1])
    copies[0].wait()
    plane(0, faces[0, n - 1], faces[0, 1])
    plane(6, faces[0, n - 1], faces[0, 0])
    behind = {p: behind[p] + faces[0, q] for p, q in ((n - 2, n - 2), (1, 2))}
    copies[3].wait()
    plane(3, faces[3, n - 1], faces[3, 0])
    plane(4, *(behind[p] + faces[3, p] * (1.0 / 3.0) for p in (n - 2, 1)))

    @pl.when(me == 1)
    def _():
        wait_planes(out, (EARLY - ODD_EARLY) * 2 * (width - 2), sem)

    @pl.when(late < bases)
    def _():
        wait_planes(out, ODD_EARLY * 2 * (width - 2), sem)

    @pl.when(me == 0)
    def _():
        inner_planes(width, bases, faces, masks, out, zeros, buf, sem)
        wait_planes(out, inner_count(layers, blocks, width), sem)


def inner_count(layers, blocks, width):
    return layers * blocks * 3 * width - 8 * blocks


def inner_planes(width, last_run, faces, masks, out, zeros, buf, sem):
    layers, blocks = buf.shape[:2]
    rows, lanes = faces.shape[2:]
    box, depth = 3 * width, width - 2
    bases = layers * blocks
    zeros[...] = jnp.zeros(zeros.shape, jnp.float32)

    for b in (0, bases):
        clear_run(zeros, out, b, bases, width, sem).start()
    clear_runs(zeros, out, 1, last_run, bases, width, sem)
    ln = Lanes((rows, lanes), width)
    plane = functools.partial(plane_at, ln, faces)

    def send(k, layer):
        start = 4 if layer == 0 else 0
        count = width + 4 - start - (4 if layer == layers - 1 else 0)
        return pltpu.make_async_copy(
            buf.at[layer, k, pl.ds(start, count)],
            out.at[pl.ds((layer * blocks + k) * box + depth + start, count)],
            sem,
        )

    def between(layer):
        base = layer * width
        ma, mb = masks[layer - 1, 0:1], masks[layer, 0:1]
        to_above, to_below = masks[layer - 1, 2:3], masks[layer, 1:2]
        a3, a2, a1 = (plane(base - i) for i in (3, 2, 1))
        b0, b1, b2 = (plane(base + i) for i in (0, 1, 2))
        a1.edge(False)
        b0.edge(True)
        low = functools.partial(store, ln, buf.at[layer - 1])
        high = functools.partial(store, ln, buf.at[layer])
        vo, vz, vx, total = second(a2, a1, a3, False, ma, to_below)
        low(width, blocks, vo, vz, total)
        high(0, blocks, vx, None, total)
        vo, vz = edge_own(a1, 1.0 - a2.z1, a2.z1, b0.x1, False, ma)
        vx, vd = edge_spill(a1, b0, False)
        total = edge_total(a1, ma)
        low(width + 1, blocks, vo, vz, total)
        high(1, blocks, vx, vd, total)
        vo, vz = edge_own(b0, 1.0 - b1.z1, b1.z1, a1.x1, True, mb)
        vx, vd = edge_spill(b0, a1, True)
        total = edge_total(b0, mb)
        high(2, blocks, vo, vz, total)
        low(width + 2, blocks, vx, vd, total)
        vo, vz, vx, total = second(b1, b0, b2, True, mb, to_above)
        high(3, blocks, vo, vz, total)
        low(width + 3, blocks, vx, None, total)

    for layer in range(layers):
        planes = [plane(layer * width + j) for j in range(1, width - 1)]
        mz = masks[layer, 0:1]
        for j in range(2, width - 2):
            vo, vz, total = middle(planes[j - 1], planes[j - 2], planes[j], mz)
            store(ln, buf.at[layer], j + 2, blocks, vo, vz, total)
        if layer < layers - 1:
            between(layer + 1)

        @pl.loop(0, blocks)
        def _(k):
            send(k, layer).start()


def bulk_kernel(width, axis, faces, masks, held, out, zeros, buf, sem):
    del held
    me = lax.axis_index(axis)
    layers, blocks = buf.shape[:2]
    bases = layers * blocks
    run = 2 * (width - 2)

    @pl.when(me != 0)
    def _():
        last_run = first_early(me, bases)
        inner_planes(width, last_run, faces, masks, out, zeros, buf, sem)
        wait_planes(out, inner_count(layers, blocks, width) - EARLY * run, sem)

    @pl.when(me > 1)
    def _():
        wait_planes(out, (EARLY - ODD_EARLY) * run, sem)

    @pl.when((me > 1) & (lax.rem(me, 2) == 0))
    def _():
        wait_planes(out, ODD_EARLY * run, sem)


def inside_kernel(blocks, axis, count, faces, masks, msg, held, side):
    del held
    me = lax.axis_index(axis)
    low = lax.rem(me, 2) == 1
    ln = Lanes(faces.shape[2:], masks.shape[2] // blocks)
    work_side(ln, low, low | (me < count - 1), faces, masks, msg, store_side(ln, side, low, blocks))


def edge_kernel(width, blocks, axis, count, faces, masks, msg, inside, held, out, side, sem):
    del held
    layers = masks.shape[0]
    me = lax.axis_index(axis)
    low = lax.rem(me, 2) == 0
    for k in range(blocks):
        send_one_side(inside, out, jnp.logical_not(low), width, layers, sem, k).start()
    ln = Lanes(faces.shape[2:], width)
    valid = jnp.where(low, me > 0, me < count - 1)
    work_side(ln, low, valid, faces, masks, msg, store_side(ln, side, low, blocks))
    for k in range(blocks):
        send_one_side(side, out, low, width, layers, sem, k).start()
    wait_planes(out, 8 * blocks, sem)


def swaps(firsts):
    return [pair for i in firsts for pair in ((i, i + 1), (i + 1, i))]


def on_device(trans_east, trans_north, trans_up, storage, support_reach, *, axis, count):
    layers, blocks, _ = support_reach.shape
    n, rows, lanes = trans_east.shape
    width = n // layers
    f32 = jnp.float32
    anywhere = pl.BlockSpec(memory_space=pl.ANY)
    vmem = pl.BlockSpec(memory_space=pltpu.VMEM)
    params = pltpu.CompilerParams(vmem_limit_bytes=16 * 2**20)
    outside = tuple(
        pltpu.with_memory_space_constraint(x, pltpu.HBM)
        for x in (trans_east, trans_north, trans_up, storage)
    )
    reach = jnp.transpose(support_reach, (0, 2, 1))
    reach = pltpu.with_memory_space_constraint(reach, pltpu.HBM)
    bases = layers * blocks
    out_shape = jax.ShapeDtypeStruct((bases * 3 * width, rows, lanes), f32)
    inner = [
        pltpu.VMEM((2 * (width - 2), rows, lanes), f32),
        pltpu.VMEM((layers, blocks, width + 4, rows, lanes), f32),
    ]
    tiles = 1 + 7 * rows // TAIL
    msg_a, msg_b, masks, faces, started = pl.pallas_call(
        functools.partial(pack_kernel, n, width, axis),
        out_shape=(
            pltpu.VMEM((tiles, TAIL, lanes), f32),
            pltpu.VMEM((tiles + 1, TAIL, lanes), f32),
            pltpu.VMEM((layers, TAIL, lanes), f32),
            pltpu.VMEM((4, n, rows, lanes), f32),
            out_shape,
        ),
        in_specs=[anywhere] * 5,
        out_specs=(vmem,) * 4 + (anywhere,),
        scratch_shapes=[
            pltpu.VMEM((layers, 4, blocks), jnp.int32),
            *inner,
            pltpu.SemaphoreType.DMA((5,)),
            pltpu.SemaphoreType.DMA,
        ],
        compiler_params=params,
        name="pack",
    )(*outside, reach)
    got_a = lax.ppermute(msg_a, axis, swaps(range(0, count - 1, 2)))
    got_b = lax.ppermute(msg_b, axis, swaps(range(1, count - 1, 2)))

    bulk = pl.pallas_call(
        functools.partial(bulk_kernel, width, axis),
        out_shape=out_shape,
        in_specs=[vmem] * 2 + [anywhere],
        out_specs=anywhere,
        scratch_shapes=inner + [pltpu.SemaphoreType.DMA],
        input_output_aliases={2: 0},
        compiler_params=params,
        cost_estimate=pl.CostEstimate(flops=10**7, bytes_accessed=7 * 10**6, transcendentals=0),
        name="bulk",
    )(faces, masks, started)
    side = pltpu.VMEM((blocks, 4, rows, lanes), f32)
    inside = pl.pallas_call(
        functools.partial(inside_kernel, blocks, axis, count),
        out_shape=side,
        in_specs=[vmem] * 3 + [anywhere],
        out_specs=vmem,
        compiler_params=params,
        cost_estimate=pl.CostEstimate(flops=10**6, bytes_accessed=10**6, transcendentals=0),
        name="inside",
    )(faces, masks, got_a, pltpu.with_memory_space_constraint(bulk, pltpu.HBM))
    out = pl.pallas_call(
        functools.partial(edge_kernel, width, blocks, axis, count),
        out_shape=out_shape,
        in_specs=[vmem] * 4 + [anywhere],
        out_specs=anywhere,
        scratch_shapes=[side, pltpu.SemaphoreType.DMA],
        input_output_aliases={4: 0},
        compiler_params=params,
        cost_estimate=pl.CostEstimate(flops=10**6, bytes_accessed=10**6, transcendentals=0),
        name="edges",
    )(faces, masks, got_b, inside, bulk)
    return out.reshape(layers, blocks, 3 * width, rows, lanes)


def solution(mesh):
    spread = P(("groups", "blk"))
    return jax.shard_map(
        functools.partial(on_device, axis="blk", count=mesh.shape["blk"]),
        mesh=mesh,
        in_specs=(spread,) * 5,
        out_specs=spread,
        check_vma=False,
    )
```

profile of v0, /device:TPU:5, one launch (start us, length us, event | category | flops | bytes accessed | tf_op | source)
XLA Modules:
  0.0 9.0 jit_solution(12337770050822032209)
XLA Ops:
  0.0 1.6 %pack.1 = (f32[15,8,128]{2,1,0:T(8,128)S(1)}, f32[16,8,128]{2,1,0:T(8,128)S(1)}, f32[2,8,128]{2,1,0:T(8,128)S(1)}, f32[4,32,16,128]{3,2,1,0:T(8,128)S(1)}, f32[768,16,128]{2,1,0:T(8,128)}) custom-call(f32[32,16,128]{2,1,0:T(8,128)} %tx.1, f32[32,16,128]{2,1,0:T(8,128)} %ty.1, f32[32,16,128]{2,1,0:T(8,128)} %tz.1, f32[32,16,128]{2,1,0:T(8,128)} %s.1, ...), custom_call_target="tpu_custom_call" | custom-call | tf_op jit(solution)/shard_map/pack/pallas_call | solution.py:470
  1.6 3.4 %collective-permute-start = (f32[16,8,128]{2,1,0:T(8,128)S(1)}, f32[16,8,128]{2,1,0:T(8,128)S(1)}, u32[]{:S(2)}, u32[]{:S(2)}) collective-permute-start(f32[16,8,128]{2,1,0:T(8,128)S(1)} %get-tuple-element.12), channel_id=1, source_target_pairs={{1,2},{2,1},{3,4},{4,3},{5,6},{6,5},{7,8},{8,7},{9,10},{10,9},{11,... | collective-permute-start | bytes 196616 | tf_op jit(solution)/shard_map/ppermute | solution.py:491
  5.0 0.1 collective-permute-start.1
  5.1 2.2 %bulk.1.held = f32[768,16,128]{2,1,0:T(8,128)} custom-call(f32[4,32,16,128]{3,2,1,0:T(8,128)S(1)} %get-tuple-element.10.faces, f32[2,8,128]{2,1,0:T(8,128)S(1)} %get-tuple-element.11.masks, f32[768,16,128]{2,1,0:T(8,128)} %get-tuple-element.14.held), custom_call_target="tpu_custom_call", output_to_operand_aliasing={{}: (2, {})} | custom-call | flops 10000000 | bytes 7000000 | tf_op jit(solution)/shard_map/bulk/pallas_call | solution.py:493
  7.3 0.0 collective-permute-done.1.msg
  7.3 0.2 %inside.1 = f32[8,4,16,128]{3,2,1,0:T(8,128)S(1)} custom-call(f32[4,32,16,128]{3,2,1,0:T(8,128)S(1)} %get-tuple-element.10.faces, f32[2,8,128]{2,1,0:T(8,128)S(1)} %get-tuple-element.11.masks, f32[15,8,128]{2,1,0:T(8,128)S(1)} %collective-permute-done.1.msg, f32[768,16,128]{2,1,0:T(8,128)} %bulk.1.held), custom_call_target="tpu_custom_call" | custom-call | flops 1000000 | bytes 1000000 | tf_op jit(solution)/shard_map/inside/pallas_call | solution.py:505
  7.5 0.6 %collective-permute-done.msg = f32[16,8,128]{2,1,0:T(8,128)S(1)} collective-permute-done((f32[16,8,128]{2,1,0:T(8,128)S(1)}, f32[16,8,128]{2,1,0:T(8,128)S(1)}, u32[]{:S(2)}, u32[]{:S(2)}) %collective-permute-start) | collective-permute-done | bytes 65568 | tf_op jit(solution)/shard_map/ppermute | solution.py:491
  8.1 0.9 %edges.1 = f32[768,16,128]{2,1,0:T(8,128)} custom-call(f32[4,32,16,128]{3,2,1,0:T(8,128)S(1)} %get-tuple-element.10.faces, f32[2,8,128]{2,1,0:T(8,128)S(1)} %get-tuple-element.11.masks, f32[16,8,128]{2,1,0:T(8,128)S(1)} %collective-permute-done.msg, f32[8,4,16,128]{3,2,1,0:T(8,128)S(1)} %inside.1, ...), custom_call_target="tpu_custom_call", output_to_operand_aliasing={{}: (4, {})} | custom-call | flops 1000000 | bytes 1000000 | tf_op jit(solution)/shard_map/edges/pallas_call | solution.py:514
Async XLA Ops:
  1.6 6.5 %collective-permute-start = (f32[16,8,128]{2,1,0:T(8,128)S(1)}, f32[16,8,128]{2,1,0:T(8,128)S(1)}, u32[]{:S(2)}, u32[]{:S(2)}) collective-permute-start(f32[16,8,128]{2,1,0:T(8,128)S(1)} %get-tuple-element.12), channel_id=1, source_target_pairs={{1,2},{2,1},{3,4},{4,3},{5,6},{6,5},{7,8},{8,7},{9,10},{10,9},{11,... | collective-permute-start | bytes 196616 | tf_op jit(solution)/shard_map/ppermute | solution.py:491
  5.0 2.3 %collective-permute-start.1 = (f32[15,8,128]{2,1,0:T(8,128)S(1)}, f32[15,8,128]{2,1,0:T(8,128)S(1)}, u32[]{:S(2)}, u32[]{:S(2)}) collective-permute-start(f32[15,8,128]{2,1,0:T(8,128)S(1)} %get-tuple-element.13), channel_id=1, source_target_pairs={{0,1},{1,0},{2,3},{3,2},{4,5},{5,4},{6,7},{7,6},{8,9},{9,8},{10,11... | collective-permute-start | bytes 184328 | tf_op jit(solution)/shard_map/ppermute | solution.py:490
where the time goes:
time: 9.16 us; the launch traced here: 8.98 us
  Pallas kernels  4.91 us (54%)
  starting transfers between devices  3.45 us (38%)
  waiting for transfers between devices  0.58 us (6%)
    ppermute x1, starting transfers between devices, on_device(): got_b = lax.ppermute(msg_b, axis, swaps(range(1, count - 1, 2)))  3.38 us
    pallas_call x1, Pallas kernels, on_device(): pl.pallas_call(functools.partial(bulk_kernel, width, axis), out_shape=out...  2.22 us
    pallas_call x1, Pallas kernels, on_device(): pl.pallas_call(functools.partial(pack_kernel, n, width, axis), out_shape=...  1.59 us
    pallas_call x1, Pallas kernels, on_device(): pl.pallas_call(functools.partial(edge_kernel, width, blocks, axis, count)...  0.9 us
    ppermute x1, waiting for transfers between devices, on_device(): got_b = lax.ppermute(msg_b, axis, swaps(range(1, count - 1, 2)))  0.57 us
    pallas_call x1, Pallas kernels, on_device(): pl.pallas_call(functools.partial(inside_kernel, blocks, axis, count), out...  0.2 us
  transfers between devices with their start and end apart: 2, of which 1 were waited for; matrix products, arithmetic and copies ran while one was open for 0% of the time, Pallas kernels for 27%

commit v1 on v0

--- a/solution.py
+++ b/solution.py
@@ -9,8 +9,7 @@
 
 
 TAIL = 8
-EARLY = 15
-ODD_EARLY = 4
+EARLY = 12
 
 
 class Lanes:
@@ -243,7 +242,7 @@
 
 
 def first_early(me, bases):
-    return jnp.where(me == 1, bases - EARLY, jnp.where(lax.rem(me, 2) == 1, bases - ODD_EARLY, bases))
+    return jnp.where(me == 1, bases - EARLY, bases)
 
 
 def pack_kernel(
@@ -263,7 +262,7 @@
     me = lax.axis_index(axis)
     late = first_early(me, bases)
 
-    @pl.when(late < bases)
+    @pl.when(me == 1)
     def _():
         zeros[...] = jnp.zeros(zeros.shape, jnp.float32)
         clear_runs(zeros, out, late, bases, bases, width, sem)
@@ -318,11 +317,7 @@
 
     @pl.when(me == 1)
     def _():
-        wait_planes(out, (EARLY - ODD_EARLY) * 2 * (width - 2), sem)
-
-    @pl.when(late < bases)
-    def _():
-        wait_planes(out, ODD_EARLY * 2 * (width - 2), sem)
+        wait_planes(out, EARLY * 2 * (width - 2), sem)
 
     @pl.when(me == 0)
     def _():
@@ -412,11 +407,7 @@
 
     @pl.when(me > 1)
     def _():
-        wait_planes(out, (EARLY - ODD_EARLY) * run, sem)
-
-    @pl.when((me > 1) & (lax.rem(me, 2) == 0))
-    def _():
-        wait_planes(out, ODD_EARLY * run, sem)
+        wait_planes(out, EARLY * run, sem)
 
 
 def inside_kernel(blocks, axis, count, faces, masks, msg, held, side):

time: 9.16 us -> 9.01 us (0.984)
  the two profiles are of different devices: /device:TPU:5 before, /device:TPU:1 now
where the time goes in v1:
time: 9.01 us; the launch traced here: 8.83 us
  Pallas kernels  4.9 us (54%)
  starting transfers between devices  3.87 us (43%)
    ppermute x1, starting transfers between devices, on_device(): got_b = lax.ppermute(msg_b, axis, swaps(range(1, count - 1, 2)))  3.8 us
    pallas_call x1, Pallas kernels, on_device(): pl.pallas_call(functools.partial(pack_kernel, n, width, axis), out_shape=...  1.99 us
    pallas_call x1, Pallas kernels, on_device(): pl.pallas_call(functools.partial(bulk_kernel, width, axis), out_shape=out...  1.79 us
    pallas_call x1, Pallas kernels, on_device(): pl.pallas_call(functools.partial(edge_kernel, width, blocks, axis, count)...  0.91 us
    pallas_call x1, Pallas kernels, on_device(): pl.pallas_call(functools.partial(inside_kernel, blocks, axis, count), out...  0.2 us
  transfers between devices with their start and end apart: 2, of which 0 were waited for; matrix products, arithmetic and copies ran while one was open for 0% of the time, Pallas kernels for 23%

profile of v1, /device:TPU:1, one launch (start us, length us, event | category | flops | bytes accessed | tf_op | source)
XLA Modules:
  0.0 8.8 jit_solution(1056138192536539339)
XLA Ops:
  0.0 2.0 %pack.1 = (f32[15,8,128]{2,1,0:T(8,128)S(1)}, f32[16,8,128]{2,1,0:T(8,128)S(1)}, f32[2,8,128]{2,1,0:T(8,128)S(1)}, f32[4,32,16,128]{3,2,1,0:T(8,128)S(1)}, f32[768,16,128]{2,1,0:T(8,128)}) custom-call(f32[32,16,128]{2,1,0:T(8,128)} %tx.1, f32[32,16,128]{2,1,0:T(8,128)} %ty.1, f32[32,16,128]{2,1,0:T(8,128)} %tz.1, f32[32,16,128]{2,1,0:T(8,128)} %s.1, ...), custom_call_target="tpu_custom_call" | custom-call | tf_op jit(solution)/shard_map/pack/pallas_call | solution.py:461
  2.0 3.8 %collective-permute-start = (f32[16,8,128]{2,1,0:T(8,128)S(1)}, f32[16,8,128]{2,1,0:T(8,128)S(1)}, u32[]{:S(2)}, u32[]{:S(2)}) collective-permute-start(f32[16,8,128]{2,1,0:T(8,128)S(1)} %get-tuple-element.12), channel_id=1, source_target_pairs={{1,2},{2,1},{3,4},{4,3},{5,6},{6,5},{7,8},{8,7},{9,10},{10,9},{11,... | collective-permute-start | bytes 196616 | tf_op jit(solution)/shard_map/ppermute | solution.py:482
  5.8 0.1 collective-permute-start.1
  5.9 1.8 %bulk.1.held = f32[768,16,128]{2,1,0:T(8,128)} custom-call(f32[4,32,16,128]{3,2,1,0:T(8,128)S(1)} %get-tuple-element.10.faces, f32[2,8,128]{2,1,0:T(8,128)S(1)} %get-tuple-element.11.masks, f32[768,16,128]{2,1,0:T(8,128)} %get-tuple-element.14.held), custom_call_target="tpu_custom_call", output_to_operand_aliasing={{}: (2, {})} | custom-call | flops 10000000 | bytes 7000000 | tf_op jit(solution)/shard_map/bulk/pallas_call | solution.py:484
  7.7 0.0 collective-permute-done.1.msg
  7.7 0.2 %inside.1 = f32[8,4,16,128]{3,2,1,0:T(8,128)S(1)} custom-call(f32[4,32,16,128]{3,2,1,0:T(8,128)S(1)} %get-tuple-element.10.faces, f32[2,8,128]{2,1,0:T(8,128)S(1)} %get-tuple-element.11.masks, f32[15,8,128]{2,1,0:T(8,128)S(1)} %collective-permute-done.1.msg, f32[768,16,128]{2,1,0:T(8,128)} %bulk.1.held), custom_call_target="tpu_custom_call" | custom-call | flops 1000000 | bytes 1000000 | tf_op jit(solution)/shard_map/inside/pallas_call | solution.py:496
  7.9 0.0 collective-permute-done.msg
  7.9 0.9 %edges.1 = f32[768,16,128]{2,1,0:T(8,128)} custom-call(f32[4,32,16,128]{3,2,1,0:T(8,128)S(1)} %get-tuple-element.10.faces, f32[2,8,128]{2,1,0:T(8,128)S(1)} %get-tuple-element.11.masks, f32[16,8,128]{2,1,0:T(8,128)S(1)} %collective-permute-done.msg, f32[8,4,16,128]{3,2,1,0:T(8,128)S(1)} %inside.1, ...), custom_call_target="tpu_custom_call", output_to_operand_aliasing={{}: (4, {})} | custom-call | flops 1000000 | bytes 1000000 | tf_op jit(solution)/shard_map/edges/pallas_call | solution.py:505
Async XLA Ops:
  2.0 5.9 %collective-permute-start = (f32[16,8,128]{2,1,0:T(8,128)S(1)}, f32[16,8,128]{2,1,0:T(8,128)S(1)}, u32[]{:S(2)}, u32[]{:S(2)}) collective-permute-start(f32[16,8,128]{2,1,0:T(8,128)S(1)} %get-tuple-element.12), channel_id=1, source_target_pairs={{1,2},{2,1},{3,4},{4,3},{5,6},{6,5},{7,8},{8,7},{9,10},{10,9},{11,... | collective-permute-start | bytes 196616 | tf_op jit(solution)/shard_map/ppermute | solution.py:482
  5.8 1.9 %collective-permute-start.1 = (f32[15,8,128]{2,1,0:T(8,128)S(1)}, f32[15,8,128]{2,1,0:T(8,128)S(1)}, u32[]{:S(2)}, u32[]{:S(2)}) collective-permute-start(f32[15,8,128]{2,1,0:T(8,128)S(1)} %get-tuple-element.13), channel_id=1, source_target_pairs={{0,1},{1,0},{2,3},{3,2},{4,5},{5,4},{6,7},{7,6},{8,9},{9,8},{10,11... | collective-permute-start | bytes 184328 | tf_op jit(solution)/shard_map/ppermute | solution.py:481

commit v2 on v1

--- a/solution.py
+++ b/solution.py
@@ -387,7 +387,7 @@
         if layer < layers - 1:
             between(layer + 1)
 
-        @pl.loop(0, blocks)
+        @pl.loop(0, blocks, unroll=True)
         def _(k):
             send(k, layer).start()
 

time: 9.01 us -> 9.3 us (1.032)
  Pallas kernels: 4.9 us -> 5.19 us
    pallas_call x1, Pallas kernels: 1.79 us -> 2.08 us  [on_device(): pl.pallas_call(functools.partial(bulk_kernel, width, axis), out_shape=out...]
  transfers between devices with their start and end apart: 2 -> 2, of which waited for: 0 -> 0; matrix products, arithmetic and copies ran while one was open for 0% -> 0% of each run, Pallas kernels for 23% -> 25%
where the time goes in v2:
time: 9.3 us; the launch traced here: 9.12 us
  Pallas kernels  5.19 us (56%)
  starting transfers between devices  3.87 us (42%)
    ppermute x1, starting transfers between devices, on_device(): got_b = lax.ppermute(msg_b, axis, swaps(range(1, count - 1, 2)))  3.8 us
    pallas_call x1, Pallas kernels, on_device(): pl.pallas_call(functools.partial(bulk_kernel, width, axis), out_shape=out...  2.08 us
    pallas_call x1, Pallas kernels, on_device(): pl.pallas_call(functools.partial(pack_kernel, n, width, axis), out_shape=...  1.99 us
    pallas_call x1, Pallas kernels, on_device(): pl.pallas_call(functools.partial(edge_kernel, width, blocks, axis, count)...  0.91 us
    pallas_call x1, Pallas kernels, on_device(): pl.pallas_call(functools.partial(inside_kernel, blocks, axis, count), out...  0.2 us
  transfers between devices with their start and end apart: 2, of which 0 were waited for; matrix products, arithmetic and copies ran while one was open for 0% of the time, Pallas kernels for 25%

profile of v2, /device:TPU:1, one launch (start us, length us, event | category | flops | bytes accessed | tf_op | source)
XLA Modules:
  0.0 9.1 jit_solution(13237898152087942324)
XLA Ops:
  0.0 2.0 %pack.1 = (f32[15,8,128]{2,1,0:T(8,128)S(1)}, f32[16,8,128]{2,1,0:T(8,128)S(1)}, f32[2,8,128]{2,1,0:T(8,128)S(1)}, f32[4,32,16,128]{3,2,1,0:T(8,128)S(1)}, f32[768,16,128]{2,1,0:T(8,128)}) custom-call(f32[32,16,128]{2,1,0:T(8,128)} %tx.1, f32[32,16,128]{2,1,0:T(8,128)} %ty.1, f32[32,16,128]{2,1,0:T(8,128)} %tz.1, f32[32,16,128]{2,1,0:T(8,128)} %s.1, ...), custom_call_target="tpu_custom_call" | custom-call | tf_op jit(solution)/shard_map/pack/pallas_call | solution.py:461
  2.0 3.8 %collective-permute-start = (f32[16,8,128]{2,1,0:T(8,128)S(1)}, f32[16,8,128]{2,1,0:T(8,128)S(1)}, u32[]{:S(2)}, u32[]{:S(2)}) collective-permute-start(f32[16,8,128]{2,1,0:T(8,128)S(1)} %get-tuple-element.12), channel_id=1, source_target_pairs={{1,2},{2,1},{3,4},{4,3},{5,6},{6,5},{7,8},{8,7},{9,10},{10,9},{11,... | collective-permute-start | bytes 196616 | tf_op jit(solution)/shard_map/ppermute | solution.py:482
  5.8 0.1 collective-permute-start.1
  5.9 2.1 %bulk.1.held = f32[768,16,128]{2,1,0:T(8,128)} custom-call(f32[4,32,16,128]{3,2,1,0:T(8,128)S(1)} %get-tuple-element.10.faces, f32[2,8,128]{2,1,0:T(8,128)S(1)} %get-tuple-element.11.masks, f32[768,16,128]{2,1,0:T(8,128)} %get-tuple-element.14.held), custom_call_target="tpu_custom_call", output_to_operand_aliasing={{}: (2, {})} | custom-call | flops 10000000 | bytes 7000000 | tf_op jit(solution)/shard_map/bulk/pallas_call | solution.py:484
  8.0 0.0 collective-permute-done.1.msg
  8.0 0.2 %inside.1 = f32[8,4,16,128]{3,2,1,0:T(8,128)S(1)} custom-call(f32[4,32,16,128]{3,2,1,0:T(8,128)S(1)} %get-tuple-element.10.faces, f32[2,8,128]{2,1,0:T(8,128)S(1)} %get-tuple-element.11.masks, f32[15,8,128]{2,1,0:T(8,128)S(1)} %collective-permute-done.1.msg, f32[768,16,128]{2,1,0:T(8,128)} %bulk.1.held), custom_call_target="tpu_custom_call" | custom-call | flops 1000000 | bytes 1000000 | tf_op jit(solution)/shard_map/inside/pallas_call | solution.py:496
  8.2 0.0 collective-permute-done.msg
  8.2 0.9 %edges.1 = f32[768,16,128]{2,1,0:T(8,128)} custom-call(f32[4,32,16,128]{3,2,1,0:T(8,128)S(1)} %get-tuple-element.10.faces, f32[2,8,128]{2,1,0:T(8,128)S(1)} %get-tuple-element.11.masks, f32[16,8,128]{2,1,0:T(8,128)S(1)} %collective-permute-done.msg, f32[8,4,16,128]{3,2,1,0:T(8,128)S(1)} %inside.1, ...), custom_call_target="tpu_custom_call", output_to_operand_aliasing={{}: (4, {})} | custom-call | flops 1000000 | bytes 1000000 | tf_op jit(solution)/shard_map/edges/pallas_call | solution.py:505
Async XLA Ops:
  2.0 6.2 %collective-permute-start = (f32[16,8,128]{2,1,0:T(8,128)S(1)}, f32[16,8,128]{2,1,0:T(8,128)S(1)}, u32[]{:S(2)}, u32[]{:S(2)}) collective-permute-start(f32[16,8,128]{2,1,0:T(8,128)S(1)} %get-tuple-element.12), channel_id=1, source_target_pairs={{1,2},{2,1},{3,4},{4,3},{5,6},{6,5},{7,8},{8,7},{9,10},{10,9},{11,... | collective-permute-start | bytes 196616 | tf_op jit(solution)/shard_map/ppermute | solution.py:482
  5.8 2.2 %collective-permute-start.1 = (f32[15,8,128]{2,1,0:T(8,128)S(1)}, f32[15,8,128]{2,1,0:T(8,128)S(1)}, u32[]{:S(2)}, u32[]{:S(2)}) collective-permute-start(f32[15,8,128]{2,1,0:T(8,128)S(1)} %get-tuple-element.13), channel_id=1, source_target_pairs={{0,1},{1,0},{2,3},{3,2},{4,5},{5,4},{6,7},{7,6},{8,9},{9,8},{10,11... | collective-permute-start | bytes 184328 | tf_op jit(solution)/shard_map/ppermute | solution.py:481
